TPU v7x, 32 devices: a whole 2x2x4 slice. The times are simulated.
32 devices in a mesh: group: 2 (over x), tensor: 16 (over z, y, core).
Axes of the slice: x: 2, y: 2, z: 4, core: 2. Of those that a mesh axis runs over, the one named last changes fastest.
Arguments:
- hidden: bfloat16 [8192, 1024], P('tensor', 'group'), parts along dimension 1, may hold values from -6 to 6
- input_conv_weight: bfloat16 [8192, 8192], P(None, 'tensor'), may hold values from -0.0625 to 0.0625
- input_gate_weight: bfloat16 [8192, 8192], P(None, 'tensor'), may hold values from -0.0625 to 0.0625
- convolution_taps: bfloat16 [4, 8192], P(None, 'tensor'), may hold values from -3 to 3
- convolution_bias: bfloat16 [8192], P('tensor'), may hold values from -3 to 3
- step_input_projection: bfloat16 [8192, 544], P('tensor'), may hold values from -0.0625 to 0.0625
- step_norm_gain: float32 [512], replicated, may hold values from 0.25 to 1.75
- step_size_projection: bfloat16 [512, 8192], P(None, 'tensor'), may hold values from -0.25 to 0.25
- step_size_bias: float32 [8192], P('tensor'), may hold values from -4 to -1
- decay_rates: float32 [16, 8192], P(None, 'tensor'), may hold values from 0.5 to 8
- skip: float32 [8192], P('tensor'), may hold values from 0.5 to 1.5
- output_weight: bfloat16 [8192, 8192], P('tensor'), may hold values from -0.09375 to 0.09375
- adapter_down_maps: bfloat16 [16, 8192, 64], P(None, 'tensor'), may hold values from -0.0625 to 0.0625
- adapter_up_maps: bfloat16 [16, 64, 8192], P(None, None, 'tensor'), may hold values from -0.75 to 0.75
- tenant: int32 [1024, 1], P('group'), parts along dimension 0, may hold values from 0 to 15; in each aligned block of 512 rows (0 to 511, 512 to 1023, ...) at most 128 rows name the same one
- convolution_cache: bfloat16 [3, 8192, 1024], P(None, 'tensor', 'group'), parts along dimension 2, may hold values from -6 to 6
- recurrent_cache: bfloat16 [16, 8192, 1024], P(None, 'tensor', 'group'), parts along dimension 2, may hold values from -6 to 6
- incoming_recurrent_states: bfloat16 [64, 16, 8192], P(('group', 'tensor')), parts along dimension 0, may hold values from -8 to 8
- incoming_conv_states: bfloat16 [64, 3, 8192], P(('group', 'tensor')), parts along dimension 0, may hold values from -8 to 8
- incoming_buffer_row: int32 [64], P('group'), parts along dimension 0, may hold values from 0 to 31, each once
- incoming_slot_index: int32 [64], P('group'), parts along dimension 0, may hold values from 0 to 511, as said below
Outputs:
- mixed: bfloat16 [8192, 1024], P('tensor', 'group'), parts along dimension 1
- ssm_next: bfloat16 [16, 8192, 1024], P(None, 'tensor', 'group'), parts along dimension 2
- conv_next: bfloat16 [3, 8192, 1024], P(None, 'tensor', 'group'), parts along dimension 2
There are 2 independent parts, one for each index of `group`. A program takes and returns all parts, laid end to end along the dimension named above; an argument that names none is the same for every part. Nothing has to cross between parts.
Inputs may be any that keep to these rules, and one draw needn't show every extreme that they name: At most 128 requests have one tenant; one tenant has exactly 128. `incoming_slot_index`: distinct request slots.
All inputs are finite; a program needn't handle non-finite values.
Results may differ from a plain program's by a relative error of at most 0.008.
Values may be sent and summed in bfloat16 or wider, within the bound.
A program may use at most 192 MiB of HBM per device.

v0:
```python
import jax
import jax.numpy as jnp
from jax import lax
from jax.sharding import PartitionSpec as P

TENANT_ROWS = 128


CONTRACT = (((0,), (0,)), ((), ()))


def slot_positions(tenant, count, capacity):
    onehot = (tenant == jnp.arange(count, dtype=jnp.int32)[None, :]).astype(jnp.int32)
    ranks = jnp.sum(jnp.cumsum(onehot, axis=0) * onehot, axis=1) - 1
    return tenant[:, 0] * capacity + ranks


def local(
    hidden,
    input_conv_weight,
    input_gate_weight,
    convolution_taps,
    convolution_bias,
    step_input_projection,
    step_norm_gain,
    step_size_projection,
    step_size_bias,
    decay_rates,
    skip,
    output_weight,
    adapter_down_maps,
    adapter_up_maps,
    tenant,
    convolution_cache,
    recurrent_cache,
    incoming_recurrent_states,
    incoming_conv_states,
    incoming_buffer_row,
    incoming_slot_index,
):
    channels = input_conv_weight.shape[1]
    dt_rank = step_size_projection.shape[0]
    states = decay_rates.shape[0]
    tenant_index_list = adapter_down_maps.shape[0]
    feature_columns_list = adapter_up_maps.shape[2]
    piece = lax.all_gather(hidden, "tensor", axis=0, tiled=True)
    x_in = lax.dot_general(input_conv_weight, piece, CONTRACT, preferred_element_type=jnp.float32)
    gate_in = lax.dot_general(
        input_gate_weight, piece, CONTRACT, preferred_element_type=jnp.float32
    )
    landed_ssm, landed_conv = (
        lax.all_to_all(
            incoming_recurrent_states, "tensor", split_axis=2, concat_axis=0, tiled=True
        ),
        lax.all_to_all(incoming_conv_states, "tensor", split_axis=2, concat_axis=0, tiled=True),
    )
    landed_ssm = jnp.take(landed_ssm, incoming_buffer_row, axis=0)
    landed_conv = jnp.take(landed_conv, incoming_buffer_row, axis=0)
    ssm_old = recurrent_cache.at[:, :, incoming_slot_index].set(
        jnp.transpose(landed_ssm, (1, 2, 0))
    )
    conv_old = convolution_cache.at[:, :, incoming_slot_index].set(
        jnp.transpose(landed_conv, (1, 2, 0))
    )
    x_low = x_in.astype(jnp.bfloat16)
    window = jnp.concatenate([conv_old, x_low[None]], axis=0)
    conv_next = window[1:]
    conv_sum = jnp.sum(
        window.astype(jnp.float32) * convolution_taps.astype(jnp.float32)[:, :, None], axis=0
    )
    u_low = jax.nn.silu(conv_sum + convolution_bias.astype(jnp.float32)[:, None]).astype(
        jnp.bfloat16
    )
    partial_mix = lax.dot_general(
        step_input_projection, u_low, CONTRACT, preferred_element_type=jnp.float32
    )
    mixing = lax.psum(partial_mix, "tensor")
    dt_low = mixing[:dt_rank]
    b_in = mixing[dt_rank : dt_rank + states]
    c_out = mixing[dt_rank + states :]
    factor = lax.rsqrt(jnp.mean(dt_low * dt_low, axis=0, keepdims=True) + 1e-06)
    dt_norm = (dt_low * factor * step_norm_gain[:, None]).astype(jnp.bfloat16)
    dt_pre = lax.dot_general(
        step_size_projection, dt_norm, CONTRACT, preferred_element_type=jnp.float32
    )
    delta = jax.nn.softplus(dt_pre + step_size_bias[:, None])
    u_full = u_low.astype(jnp.float32)
    state = (
        jnp.exp(-delta[None] * decay_rates[:, :, None]) * ssm_old.astype(jnp.float32)
        + (delta * u_full)[None] * b_in[:, None, :]
    )
    ssm_next = state.astype(jnp.bfloat16)
    y_ssm = jnp.sum(state * c_out[:, None, :], axis=0)
    y_low = ((y_ssm + skip[:, None] * u_full) * jax.nn.silu(gate_in)).astype(jnp.bfloat16)
    slot_index = slot_positions(tenant, tenant_index_list, TENANT_ROWS)
    output_padded = (
        jnp.zeros((channels, tenant_index_list * TENANT_ROWS), jnp.bfloat16)
        .at[:, slot_index]
        .set(y_low)
    )
    output_padded = output_padded.reshape(channels, tenant_index_list, TENANT_ROWS)
    value_portion = jnp.einsum(
        "wuv,uwg->guv", output_padded, adapter_down_maps, preferred_element_type=jnp.float32
    )
    value_lowrank = lax.psum(value_portion, "tensor").astype(jnp.bfloat16)
    adapter_index = jnp.einsum(
        "ysl,sym->msl", value_lowrank, adapter_up_maps, preferred_element_type=jnp.float32
    )
    adapter_index = jnp.take(
        adapter_index.reshape(feature_columns_list, tenant_index_list * TENANT_ROWS),
        slot_index,
        axis=1,
    )
    main = lax.psum_scatter(
        lax.dot_general(output_weight, y_low, CONTRACT, preferred_element_type=jnp.float32),
        "tensor",
        scatter_dimension=0,
        tiled=True,
    )
    mixed = (main + adapter_index).astype(jnp.bfloat16)
    return (mixed, ssm_next, conv_next)


def solution(mesh):
    placed = (
        P("tensor", "group"),
        P(None, "tensor"),
        P(None, "tensor"),
        P(None, "tensor"),
        P("tensor"),
        P("tensor", None),
        P(),
        P(None, "tensor"),
        P("tensor"),
        P(None, "tensor"),
        P("tensor"),
        P("tensor", None),
        P(None, "tensor", None),
        P(None, None, "tensor"),
        P("group", None),
        P(None, "tensor", "group"),
        P(None, "tensor", "group"),
        P(("group", "tensor"), None, None),
        P(("group", "tensor"), None, None),
        P("group"),
        P("group"),
    )
    return jax.shard_map(
        local,
        mesh=mesh,
        in_specs=placed,
        out_specs=(P("tensor", "group"), P(None, "tensor", "group"), P(None, "tensor", "group")),
        check_vma=False,
    )
```

profile of v0, /device:TPU:0, one launch (start us, length us, event | category | flops | bytes accessed | tf_op | source)
XLA Modules:
  0.0 440.5 jit_solution(4865484350609502408)
XLA Ops:
  7.9 8.3 %copy.80 = bf16[2,3,8192]{1,0,2:T(2,128)(2,1)} copy(bf16[2,3,8192]{2,0,1:T(2,128)(2,1)} %param.39) | data formatting | bytes 196608 | tf_op args[18]
  16.3 7.5 %reshape.127 = bf16[16,2,1536]{2,1,0:T(2,128)(2,1)} reshape(bf16[8192,2,3]{2,1,0:T(2,128)(2,1)} %bitcast.77) | data formatting | bytes 196608
  23.7 7.4 %all-to-all-start = ((bf16[16,2,1536]{2,1,0:T(2,128)(2,1)}), bf16[16,2,1536]{2,1,0:T(2,128)(2,1)S(1)}, u32[]{:S(2)}, u32[]{:S(2)}) async-start(bf16[16,2,1536]{2,1,0:T(2,128)(2,1)} %reshape.127), calls=%async_computation | async-start | bytes 196608 | tf_op jit(solution)/shard_map/all_to_all | solution.py:55
  31.2 3.2 copy.83
  34.4 8.6 %copy.85 = bf16[2,16,8192]{1,0,2:T(2,128)(2,1)} copy(bf16[2,16,8192]{2,1,0:T(8,128)(2,1)} %param.38) | data formatting | bytes 1048576 | tf_op args[17]
  43.0 6.4 %reshape.125 = bf16[16,2,8192]{2,1,0:T(2,128)(2,1)} reshape(bf16[8192,2,16]{2,1,0:T(2,128)(2,1)} %bitcast.75) | data formatting | bytes 1048576
  49.5 6.1 %all-to-all-start.1 = ((bf16[16,2,8192]{2,1,0:T(2,128)(2,1)}), bf16[16,2,8192]{2,1,0:T(2,128)(2,1)}, u32[]{:S(2)}, u32[]{:S(2)}) async-start(bf16[16,2,8192]{2,1,0:T(2,128)(2,1)} %reshape.125), calls=%async_computation.1 | async-start | bytes 1048576 | tf_op jit(solution)/shard_map/all_to_all | solution.py:52
  55.8 9.8 %reshape.128 = bf16[8192,2,3]{2,1,0:T(2,128)(2,1)} reshape(bf16[16,2,1536]{2,1,0:T(2,128)(2,1)S(1)} %all-to-all-done) | data formatting | bytes 196608
  65.6 9.7 %copy.100 = bf16[16,2,3,512]{3,2,1,0:T(4,128)(2,1)S(1)} copy(bf16[16,2,3,512]{2,1,3,0:T(2,128)(2,1)} %bitcast.76) | data formatting | bytes 196608 | tf_op jit(solution)/shard_map/all_to_all | solution.py:55
  77.6 21.0 %all-gather.2.cloned.1.call-done = bf16[8192,512]{1,0:T(8,128)(2,1)} async-done(((bf16[512,512]{1,0:T(8,128)(2,1)}), bf16[8192,512]{1,0:T(8,128)(2,1)}) %all-gather.2.cloned.1.call-update) | async-done | bytes 8388624 | tf_op jit(solution)/shard_map/all_gather | solution.py:46
  98.6 11.1 %fusion.3 = bf16[1,512,512]{2,1,0:T(8,128)(2,1)} fusion(bf16[8192,512]{1,0:T(8,128)(2,1)} %param.22, bf16[8192,512]{1,0:T(8,128)(2,1)} %all-gather.2.cloned.1.call-done), kind=kOutput, calls=%fused_computation.22 | convolution fusion | flops 4295229440 | bytes 17301504 | tf_op jit(solution)/shard_map/dot_general | solution.py:47
  109.7 3.6 copy.84
  113.3 5.6 %multiply_reduce_fusion.1 = f32[512,512]{0,1:T(8,128)S(1)} fusion(bf16[1,512,512]{1,0,2:T(2,128)(2,1)} %copy.84, f32[4,512]{1,0:T(4,128)S(1)} %convert_element_type.43, bf16[3,512,512]{1,0,2:T(4,128)(2,1)S(1)} %scatter_fusion), kind=kLoop, calls=%fused_computation.10 | loop fusion | flops 6029312 | bytes 3153920 | tf_op jit(solution)/shard_map/reduce_sum | solution.py:68
  121.8 14.9 %copy.88 = bf16[16,512,512]{1,0,2:T(8,128)(2,1)} copy(bf16[16,512,512]{2,1,0:T(8,128)(2,1)} %param.37) | data formatting | bytes 16777216 | tf_op args[16]
  136.7 5.3 %reshape.126 = bf16[8192,2,16]{2,1,0:T(2,128)(2,1)} reshape(bf16[16,2,8192]{2,1,0:T(2,128)(2,1)} %all-to-all-done.1) | data formatting | bytes 1048576
  142.0 10.3 %copy.102 = bf16[2,16,16,512]{3,1,0,2:T(8,128)(2,1)} copy(bf16[2,16,16,512]{1,0,3,2:T(2,128)(2,1)} %bitcast.74) | data formatting | bytes 1048576 | tf_op jit(solution)/shard_map/all_to_all | solution.py:52
  152.3 2.5 gather_fusion.1
  156.7 4.8 %scatter_fusion.1 = bf16[16,512,512]{1,0,2:T(8,128)(2,1)} fusion(bf16[16,512,512]{1,0,2:T(8,128)(2,1)} %copy.88, s32[32]{0:T(128)S(1)} %compare_select_fusion.3, bf16[32,16,512]{2,1,0:T(8,128)(2,1)} %broadcast_select_fusion), kind=kCustom, calls=%fused_computation.4 | custom fusion | bytes 1572992 | tf_op jit(solution)/shard_map/scatter | solution.py:59
  161.6 51.7 %all-reduce.3.cloned.1.call-done = f32[544,512]{1,0:T(8,128)} async-done(((f32[544,512]{1,0:T(8,128)}), f32[544,512]{1,0:T(8,128)}) %all-reduce.3.cloned.1.call-update) | async-done | bytes 1114128 | tf_op jit(solution)/shard_map/psum | solution.py:77
  216.4 3.1 fusion.19
  220.5 8.5 %fusion = (bf16[16,512,512]{1,0,2:T(8,128)(2,1)}, f32[512,512]{0,1:T(8,128)S(1)}) fusion(bf16[16,512,512]{1,0,2:T(8,128)(2,1)S(1)} %copy-done.1, f32[16,512]{0,1:T(8,128)S(1)} %copy.89, f32[512,512]{0,1:T(8,128)S(1)} %get-tuple-element.25, f32[16,512]{1,0:T(8,128)S(1)} %copy-done.6, f32[512,512]{0,1:T(8,128)S(1)} %get-tuple-element.24, f32[16,512]{0,1:T(8,128)S(1)} %copy-done.3), kind=kLoop, calls=%fused_computation.8 | loop fusion | flops 33292288 | bytes 20021248 | tf_op jit(solution)/shard_map/convert_element_type | solution.py:92
  229.0 10.8 %fusion.6 = bf16[512,512]{0,1:T(8,128)(2,1)S(1)} fusion(f32[512,512]{0,1:T(8,128)S(1)} %get-tuple-element.21, f32[512]{0:T(512)S(1)} %copy-done.13, f32[512,512]{0,1:T(8,128)S(1)} %copy-done.5, f32[512]{0:T(512)S(1)} %convert_element_type.44, bf16[8192,512]{1,0:T(8,128)(2,1)} %param.23, bf16[8192,512]{1,0:T(8,128)(2,1)} %all-gather.2.cloned.1.call-done), kind=kOutput, calls=%fused_computation.25 | convolution fusion | flops 4298899456 | bytes 19402752 | tf_op jit(solution)/shard_map/dot_general | solution.py:48
  240.7 8.0 %convolution_bitcast_fusion = f32[8192,512]{0,1:T(8,128)} fusion(bf16[512,512]{0,1:T(8,128)(2,1)S(1)} %fusion.6, bf16[512,8192]{1,0:T(8,128)(2,1)S(1)} %bitcast.73), kind=kOutput, calls=%fused_computation.9 | convolution fusion | flops 4294967296 | bytes 25690112 | tf_op jit(solution)/shard_map/dot_general | solution.py:115
  251.0 5.0 %fusion.1 = bf16[3,512,512]{1,0,2:T(4,128)(2,1)} fusion(bf16[1,512,512]{1,0,2:T(2,128)(2,1)} %copy.84, bf16[3,512,512]{1,0,2:T(4,128)(2,1)S(1)} %scatter_fusion), kind=kLoop, calls=%fused_computation.14 | loop fusion | flops 3145728 | bytes 3670016 | tf_op jit(solution)/shard_map/concatenate | solution.py:66
  256.0 4.3 copy.97
  260.3 14.8 %copy.96 = bf16[16,512,512]{2,1,0:T(8,128)(2,1)} copy(bf16[16,512,512]{1,0,2:T(8,128)(2,1)} %get-tuple-element.20) | data formatting | bytes 16777216
  275.1 3.7 scatter_custom_fusion.2
  278.8 2.8 convolution_bitcast_fusion.2
  281.6 78.4 %all-reduce.4 = bf16[64,16,128]{2,0,1:T(8,128)(2,1)S(1)} all-reduce(f32[64,16,128]{2,0,1:T(8,128)} %convolution_bitcast_fusion.2), channel_id=1, replica_groups=mesh['group'=2,'tensor'=16] {'tensor'}, use_global_device_ids=true, to_apply=%region_11.12 | all-reduce | flops 131072 | bytes 786432 | tf_op jit(solution)/shard_map/psum | solution.py:105
  360.0 2.7 fusion.20
  362.7 4.2 gather_fusion.2
  366.9 64.6 %reduce-scatter.2.cloned.1.call-done = f32[512,512]{0,1:T(8,128)} async-done(((f32[8192,512]{0,1:T(8,128)}), f32[512,512]{0,1:T(8,128)}) %reduce-scatter.2.cloned.1.call-update) | async-done | bytes 1048592 | tf_op jit(solution)/shard_map/reduce_scatter | solution.py:114
  (72 shorter events, 17.7 us)
Async XLA Ops:
  7.2 352.8 %copy-start = (bf16[16,64,512]{2,1,0:T(8,128)(2,1)S(1)}, bf16[16,64,512]{2,1,0:T(8,128)(2,1)}, u32[]{:S(2)}) copy-start(bf16[16,64,512]{2,1,0:T(8,128)(2,1)} %param.34) | copy-start | bytes 3145732
  7.2 91.5 %all-gather.2.cloned.1.call-start = ((), (), s32[]{:S(2)}) async-start(), calls=%async_computation.3 | async-start | bytes 8912896 | tf_op jit(solution)/shard_map/all_gather | solution.py:46
  7.9 23.2 %copy-start.9 = (bf16[512]{0:T(512)(128)(2,1)S(1)}, bf16[512]{0:T(512)(128)(2,1)}, u32[]{:S(2)}) copy-start(bf16[512]{0:T(512)(128)(2,1)} %param.25) | copy-start | bytes 3076
  7.9 23.2 %copy-start.8 = (bf16[4,512]{1,0:T(4,128)(2,1)S(1)}, bf16[4,512]{1,0:T(4,128)(2,1)}, u32[]{:S(2)}) copy-start(bf16[4,512]{1,0:T(4,128)(2,1)} %param.24) | copy-start | bytes 12292
  23.7 25.8 %all-to-all-start = ((bf16[16,2,1536]{2,1,0:T(2,128)(2,1)}), bf16[16,2,1536]{2,1,0:T(2,128)(2,1)S(1)}, u32[]{:S(2)}, u32[]{:S(2)}) async-start(bf16[16,2,1536]{2,1,0:T(2,128)(2,1)} %reshape.127), calls=%async_computation | async-start | bytes 196608 | tf_op jit(solution)/shard_map/all_to_all | solution.py:55
  34.4 15.0 %copy-start.14 = (s32[32]{0:T(128)S(1)}, s32[32]{0:T(128)}, u32[]{:S(2)}) copy-start(s32[32]{0:T(128)} %param.40) | copy-start | bytes 388
  34.4 15.0 %copy-start.15 = (s32[32]{0:T(128)S(1)}, s32[32]{0:T(128)}, u32[]{:S(2)}) copy-start(s32[32]{0:T(128)} %param.41) | copy-start | bytes 388
  49.5 87.2 %all-to-all-start.1 = ((bf16[16,2,8192]{2,1,0:T(2,128)(2,1)}), bf16[16,2,8192]{2,1,0:T(2,128)(2,1)}, u32[]{:S(2)}, u32[]{:S(2)}) async-start(bf16[16,2,8192]{2,1,0:T(2,128)(2,1)} %reshape.125), calls=%async_computation.1 | async-start | bytes 1048576 | tf_op jit(solution)/shard_map/all_to_all | solution.py:52
  55.6 157.7 %all-reduce.3.cloned.1.call-start = ((), (), s32[]{:S(2)}) async-start(), calls=%async_computation.4 | async-start | bytes 2228224 | tf_op jit(solution)/shard_map/psum | solution.py:77
  113.3 6.6 %copy-start.10 = (bf16[512,544]{0,1:T(8,128)(2,1)S(1)}, bf16[512,544]{0,1:T(8,128)(2,1)}, u32[]{:S(2)}) copy-start(bf16[512,544]{0,1:T(8,128)(2,1)} %param.26) | copy-start | bytes 1671172
  119.0 1.0 copy-start.4
  121.5 310.0 %reduce-scatter.2.cloned.1.call-start = ((), (), s32[]{:S(2)}) async-start(), calls=%async_computation.5 | async-start | bytes 17825792 | tf_op jit(solution)/shard_map/reduce_scatter | solution.py:114
  142.0 74.3 %copy-start.11 = (f32[512]{0:T(512)S(1)}, f32[512]{0:T(512)}, u32[]{:S(2)}) copy-start(f32[512]{0:T(512)} %param.29) | copy-start | bytes 6148
  142.0 74.3 %copy-start.12 = (f32[512]{0:T(512)S(1)}, f32[512]{0:T(512)}, u32[]{:S(2)}) copy-start(f32[512]{0:T(512)} %param.27) | copy-start | bytes 6148
  216.3 4.2 copy-start.1
  216.3 4.2 copy-start.3
  216.4 4.2 copy-start.6
  220.5 8.5 %copy-start.5 = (f32[512,512]{0,1:T(8,128)S(1)}, f32[512,512]{0,1:T(8,128)}, u32[]{:S(2)}) copy-start(f32[512,512]{0,1:T(8,128)} %copy-done.4) | copy-start | bytes 3145732
  220.5 8.5 %copy-start.13 = (f32[512]{0:T(512)S(1)}, f32[512]{0:T(512)}, u32[]{:S(2)}) copy-start(f32[512]{0:T(512)} %param.31) | copy-start | bytes 6148
  220.5 20.2 %slice-start = ((s8[8388608]{0:T(1024)(128)(4,1)}), s8[4194304]{0:T(1024)(128)(4,1)S(1)}, s32[]{:S(2)}) async-start(s8[8388608]{0:T(1024)(128)(4,1)} %bitcast.72), calls=%async_computation.6 | async-start | bytes 8388608
  229.0 11.6 %slice-start.1 = ((s8[8388608]{0:T(1024)(128)(4,1)}), s8[4194304]{0:T(1024)(128)(4,1)S(1)}, s32[]{:S(2)}) async-start(s8[8388608]{0:T(1024)(128)(4,1)} %bitcast.72), calls=%async_computation.7 | async-start | bytes 8388608
  239.9 0.8 copy-start.2
  248.7 0.7 copy-start.7
Sparse Core Ops, SparseCore 0:
  10.2 88.4 all-gather.1
  121.7 91.5 all-reduce.2
  248.9 182.6 reduce-scatter.1
where the time goes:
time: 444 us; the launch traced here: 440 us
  waiting for transfers between devices  138 us (31%)
  local copies, waits for them, and re-layouts  131 us (30%)
  blocking collectives  78.4 us (18%)
  matrix products  40.2 us (9%)
  other arithmetic  25.3 us (6%)
  starting transfers between devices  14 us (3%)
  between operations  14 us (3%)
    unnamed x47, local copies, waits for them, and re-layouts  87.6 us
    psum x1, blocking collectives, local(): value_lowrank = lax.psum(value_portion, 'tensor').astype(jnp.bfloat16)  78.4 us
    reduce_scatter x1, waiting for transfers between devices, local(): lax.psum_scatter(lax.dot_general(output_weight, y_low, CONTRACT, preferre...  64.6 us
    psum x1, waiting for transfers between devices, local(): mixing = lax.psum(partial_mix, 'tensor')  51.7 us
    all_gather x1, waiting for transfers between devices, local(): piece = lax.all_gather(hidden, 'tensor', axis=0, tiled=True)  21 us
    dot_general x1, matrix products, local(): lax.dot_general(input_conv_weight, piece, CONTRACT, preferred_element_typ...  11.1 us
    dot_general x1, matrix products, local(): lax.dot_general(input_gate_weight, piece, CONTRACT, preferred_element_typ...  10.8 us
    all_to_all x1, local copies, waits for them, and re-layouts, local(): lax.all_to_all(incoming_recurrent_states, 'tensor', split_axis=2, concat_...  10.3 us
  transfers between devices with their start and end apart: 5, of which 3 were waited for; matrix products, arithmetic and copies ran while one was open for 36% of the time, Pallas kernels for 0%

commit v1 on v0

v1 whole, which is shorter than its diff:
```python
import functools

import jax
import jax.numpy as jnp
from jax import lax
from jax.experimental import pallas as pl
from jax.experimental.pallas import tpu as pltpu
from jax.sharding import PartitionSpec as P

F32 = jnp.float32
BF16 = jnp.bfloat16
CONTRACT = (((0,), (0,)), ((), ()))
ANY = pl.BlockSpec(memory_space=pl.ANY)
VM = pl.BlockSpec(memory_space=pltpu.VMEM)
DMA = pltpu.SemaphoreType.DMA
LIMIT = 56 * 1024 * 1024


def dot0(a, b):
    return lax.dot_general(a, b, CONTRACT, preferred_element_type=F32)


def remote(src, dst, send, recv, peer):
    return pltpu.make_async_remote_copy(
        src_ref=src,
        dst_ref=dst,
        send_sem=send,
        recv_sem=recv,
        device_id={"tensor": peer},
        device_id_type=pl.DeviceIdType.MESH,
    )


def greet_all(me, n):
    barrier = pltpu.get_barrier_semaphore()

    @pl.loop(1, n)
    def _(d):
        pl.semaphore_signal(
            barrier,
            inc=1,
            device_id={"tensor": lax.rem(me + d, n)},
            device_id_type=pl.DeviceIdType.MESH,
        )

    pl.semaphore_wait(barrier, n - 1)


class Ring:
    def __init__(self, n, snake):
        self.n, self.m, self.snake = n, n // 2, snake
        self.me = lax.axis_index("tensor")
        self.core = lax.rem(self.me, 2)
        chip = self.me // 2
        if snake:
            level, side = chip // 2, lax.rem(chip, 2)
            self.pos = jnp.where(side == 0, level, self.m - 1 - level)
        else:
            self.pos = chip
        self.sibling = self.me + 1 - 2 * self.core

    def at(self, offset, core=None):
        m = self.m
        pos = lax.rem(self.pos + offset + 2 * m, m)
        if self.snake:
            chip = jnp.where(pos < m // 2, 2 * pos, 2 * (m - 1 - pos) + 1)
        else:
            chip = pos
        return chip * 2 + (self.core if core is None else core)


def gather_kernel(n, snake, h_ref, wx_hbm, wg_hbm, ssm_hbm, conv_hbm, x_ref, g_ref, ssm_out,
                  conv_out, gath, wx, wg, wsem, own_sem, rs, rr, ls, lr, ss, sr, as_, ar, cs, cr):
    ring = Ring(n, snake)
    me, m, h = ring.me, ring.m, ring.m // 2
    rows = h_ref.shape[0]
    half = rows // 2
    first, second = pl.ds(0, half), pl.ds(half, half)
    cx = pltpu.make_async_copy(wx_hbm, wx, wsem.at[0])
    cg = pltpu.make_async_copy(wg_hbm, wg, wsem.at[1])
    own = pltpu.make_async_copy(h_ref, gath.at[me], own_sem.at[0])
    own.start()
    cx.start()
    cg.start()
    width = ssm_out.shape[-1]
    keep_ssm = pltpu.make_async_copy(
        ssm_hbm.at[:, :, pl.ds(pl.multiple_of(me * width, width), width)], ssm_out.at[me],
        own_sem.at[1])
    keep_conv = pltpu.make_async_copy(conv_hbm.at[me], conv_out.at[me], own_sem.at[2])
    keep_ssm.start()
    keep_conv.start()
    x_ref[...] = jnp.zeros_like(x_ref)
    g_ref[...] = jnp.zeros_like(g_ref)
    own.wait()
    greet_all(me, n)
    right, left = ring.at(1), ring.at(-1)

    def to_right(s):
        b = gath.at[ring.at(-s)]
        return remote(b, b, rs.at[s], rr.at[s], right)

    def to_left(s):
        b = gath.at[ring.at(s)]
        return remote(b, b, ls.at[s], lr.at[s], left)

    def right_half():
        b = gath.at[ring.at(1 - h), first]
        return remote(b, b, rs.at[h - 1], rr.at[h - 1], right)

    def left_half():
        b = gath.at[ring.at(h - 1), second]
        return remote(b, b, ls.at[h - 1], lr.at[h - 1], left)

    def to_sibling(k, t):
        b = gath.at[t]
        return remote(b, b, ss.at[k], sr.at[k], ring.sibling)

    def peer_copies(d):
        t = lax.rem(me + d, n)
        return (
            remote(ssm_hbm.at[:, :, pl.ds(pl.multiple_of(t * width, width), width)],
                   ssm_out.at[me], as_.at[d], ar.at[d], t),
            remote(conv_hbm.at[t], conv_out.at[me], cs.at[d], cr.at[d], t),
        )

    def compute(t):
        block = gath[t]
        k = pl.ds(pl.multiple_of(t * rows, rows), rows)
        x_ref[...] += dot0(wx[k, :], block)
        g_ref[...] += dot0(wg[k, :], block)

    other = 1 - ring.core
    to_right(0).start()
    to_left(0).start()
    to_sibling(0, me).start()

    @pl.loop(1, n)
    def _(d):
        for c in peer_copies(d):
            c.start()

    cx.wait()
    cg.wait()
    compute(me)
    to_sibling(0, ring.sibling).wait_recv()
    compute(ring.sibling)

    def step(s, last):
        a, b = ring.at(-1 - s), ring.at(1 + s)
        remote(gath.at[a], gath.at[a], rs.at[s], rr.at[s], right).wait_recv()
        remote(gath.at[b], gath.at[b], ls.at[s], lr.at[s], left).wait_recv()
        if last:
            right_half().start()
            left_half().start()
        else:
            to_right(s + 1).start()
            to_left(s + 1).start()
        to_sibling(1 + 2 * s, a).start()
        to_sibling(2 + 2 * s, b).start()
        compute(a)
        compute(b)
        a2, b2 = ring.at(-1 - s, other), ring.at(1 + s, other)
        to_sibling(1 + 2 * s, a2).wait_recv()
        compute(a2)
        to_sibling(2 + 2 * s, b2).wait_recv()
        compute(b2)

    @pl.loop(0, h - 2)
    def _(s):
        step(s, False)

    step(h - 2, True)
    far, far2 = ring.at(h), ring.at(h, other)
    b = gath.at[far, first]
    remote(b, b, rs.at[h - 1], rr.at[h - 1], right).wait_recv()
    b = gath.at[far, second]
    remote(b, b, ls.at[h - 1], lr.at[h - 1], left).wait_recv()
    to_sibling(m - 1, far).start()
    compute(far)
    to_sibling(m - 1, far2).wait_recv()
    compute(far2)

    @pl.loop(0, h - 1)
    def _(s):
        to_right(s).wait_send()
        to_left(s).wait_send()
        to_sibling(1 + 2 * s, ring.at(-1 - s)).wait_send()
        to_sibling(2 + 2 * s, ring.at(1 + s)).wait_send()

    right_half().wait_send()
    left_half().wait_send()
    to_sibling(0, me).wait_send()
    to_sibling(m - 1, far).wait_send()
    keep_ssm.wait()
    keep_conv.wait()

    @pl.loop(1, n)
    def _(d):
        t = lax.rem(me + n - d, n)
        for c in peer_copies(d):
            c.wait_send()
        remote(ssm_out.at[t], ssm_out.at[t], as_.at[d], ar.at[d], t).wait_recv()
        remote(conv_out.at[t], conv_out.at[t], cs.at[d], cr.at[d], t).wait_recv()


def mix_kernel(n, rank, part_ref, gain_ref, dt_ref, bc_ref, recv, s1, r1, s2, r2, s3, r3):
    me = lax.axis_index("tensor")
    greet_all(me, n)

    @pl.loop(1, n)
    def _(d):
        t = lax.rem(me + d, n)
        remote(part_ref.at[t], recv.at[d], s1.at[d], r1.at[d], t).start()

    recv[0] = part_ref[me]

    @pl.loop(1, n)
    def _(d):
        remote(part_ref.at[0], recv.at[d], s1.at[d], r1.at[d], lax.rem(me + d, n)).wait()

    total = jnp.sum(recv[...].astype(F32), axis=0)
    dt = total[:, :rank]
    factor = lax.rsqrt(jnp.mean(dt * dt, axis=1, keepdims=True) + 1e-06)
    dt_ref[me] = (dt * factor * gain_ref[...]).astype(BF16)
    bc_ref[me] = total[:, rank:]

    @pl.loop(1, n)
    def _(d):
        t = lax.rem(me + d, n)
        remote(dt_ref.at[me], dt_ref.at[me], s2.at[d], r2.at[d], t).start()
        remote(bc_ref.at[me], bc_ref.at[me], s3.at[d], r3.at[d], t).start()

    @pl.loop(1, n)
    def _(d):
        t = lax.rem(me + n - d, n)
        remote(dt_ref.at[t], dt_ref.at[t], s2.at[d], r2.at[d], t).wait()
        remote(bc_ref.at[t], bc_ref.at[t], s3.at[d], r3.at[d], t).wait()


def scatter_kernel(n, snake, y_ref, w_hbm, v_ref, out_ref, v_out, w, acc, sbuf, rbuf, rsend, rrecv,
                   lsend, lrecv, vrecv, wsem, rs, rr, ls, lr, ss, sr, s1, r1, s2, r2):
    ring = Ring(n, snake)
    me, m, h = ring.me, ring.m, ring.m // 2
    rows = out_ref.shape[0]
    half = rows // 2
    first, second = pl.ds(0, half), pl.ds(half, half)
    cw = pltpu.make_async_copy(w_hbm, w, wsem.at[0])
    cw.start()
    greet_all(me, n)
    right, left = ring.at(1), ring.at(-1)
    other = 1 - ring.core

    @pl.loop(1, n)
    def _(d):
        t = lax.rem(me + d, n)
        remote(v_ref.at[t], vrecv.at[d], s1.at[d], r1.at[d], t).start()

    vrecv[0] = v_ref[me]
    cw.wait()

    def part(t):
        return dot0(w[:, pl.ds(pl.multiple_of(t * rows, rows), rows)], y_ref[...])

    def sib(k):
        return remote(sbuf.at[k], rbuf.at[k], ss.at[k], sr.at[k], ring.sibling)

    def give(k, offset):
        sbuf[k] = part(ring.at(offset, other)).astype(BF16)
        sib(k).start()

    def take(k, offset):
        acc[...] = part(ring.at(offset))
        sib(k).wait_recv()
        acc[...] += rbuf[k].astype(F32)

    def going(s, to_right):
        if to_right:
            return remote(rsend.at[s], rrecv.at[s], rs.at[s], rr.at[s], right)
        return remote(lsend.at[s], lrecv.at[s], ls.at[s], lr.at[s], left)

    def start_half(to_right):
        if to_right:
            return remote(rsend.at[0, first], rrecv.at[0, first], rs.at[0], rr.at[0], right)
        return remote(lsend.at[0, second], lrecv.at[0, second], ls.at[0], lr.at[0], left)

    give(0, h)
    take(0, h)
    rsend[0, first] = acc[first].astype(BF16)
    start_half(True).start()
    lsend[0, second] = acc[second].astype(BF16)
    start_half(False).start()

    give(1, h - 1)
    give(2, 1 - h)
    take(1, h - 1)
    start_half(True).wait_recv()
    rsend[1, first] = (acc[first] + rrecv[0, first].astype(F32)).astype(BF16)
    rsend[1, second] = acc[second].astype(BF16)
    going(1, True).start()
    take(2, 1 - h)
    start_half(False).wait_recv()
    lsend[1, second] = (acc[second] + lrecv[0, second].astype(F32)).astype(BF16)
    lsend[1, first] = acc[first].astype(BF16)
    going(1, False).start()

    @pl.loop(1, n)
    def _(d):
        remote(v_ref.at[0], vrecv.at[d], s1.at[d], r1.at[d], lax.rem(me + d, n)).wait()

    v_out[me] = jnp.sum(vrecv[...], axis=0).astype(BF16)

    @pl.loop(1, n)
    def _(d):
        remote(v_out.at[me], v_out.at[me], s2.at[d], r2.at[d], lax.rem(me + d, n)).start()

    @pl.loop(2, h)
    def _(s):
        give(2 * s - 1, h - s)
        give(2 * s, s - h)
        take(2 * s - 1, h - s)
        going(s - 1, True).wait_recv()
        rsend[s] = (acc[...] + rrecv[s - 1].astype(F32)).astype(BF16)
        going(s, True).start()
        take(2 * s, s - h)
        going(s - 1, False).wait_recv()
        lsend[s] = (acc[...] + lrecv[s - 1].astype(F32)).astype(BF16)
        going(s, False).start()

    give(m - 1, 0)
    take(m - 1, 0)
    going(h - 1, True).wait_recv()
    going(h - 1, False).wait_recv()
    out_ref[...] = acc[...] + rrecv[h - 1].astype(F32) + lrecv[h - 1].astype(F32)

    start_half(True).wait_send()
    start_half(False).wait_send()

    @pl.loop(1, h)
    def _(s):
        going(s, True).wait_send()
        going(s, False).wait_send()

    @pl.loop(0, m)
    def _(k):
        sib(k).wait_send()

    @pl.loop(1, n)
    def _(d):
        t = lax.rem(me + n - d, n)
        remote(v_out.at[t], v_out.at[t], s2.at[d], r2.at[d], t).wait()


def conv_kernel(x_ref, cache_ref, land_ref, pick_ref, hit_ref, taps_ref, bias_ref, next_ref, u_ref):
    hit = hit_ref[...] > 0
    total = bias_ref[...]
    count = cache_ref.shape[0]
    for k in range(count):
        placed = dot0(land_ref[k], pick_ref[...])
        old = jnp.where(hit, placed, cache_ref[k].astype(F32))
        total = total + old * taps_ref[:, k : k + 1]
        if k > 0:
            next_ref[k - 1] = old.astype(BF16)
    low = x_ref[...].astype(BF16)
    next_ref[count - 1] = low
    total = total + low.astype(F32) * taps_ref[:, count : count + 1]
    u_ref[...] = (total / (1.0 + jnp.exp(-total))).astype(BF16)


def state_kernel(dt_ref, proj_ref, bias_ref, decay_ref, skip_ref, u_ref, gate_ref, b_ref, c_ref,
                 cache_ref, land_ref, pick_ref, hit_ref, next_ref, y_ref):
    pre = dot0(proj_ref[...], dt_ref[...]) + bias_ref[...]
    delta = jnp.maximum(pre, 0.0) + jnp.log1p(jnp.exp(-jnp.abs(pre)))
    u = u_ref[...].astype(F32)
    du = delta * u
    hit = hit_ref[...] > 0
    total = skip_ref[...] * u
    for k in range(cache_ref.shape[0]):
        placed = dot0(land_ref[k], pick_ref[...])
        old = jnp.where(hit, placed, cache_ref[k].astype(F32))
        state = jnp.exp(-delta * decay_ref[:, k : k + 1]) * old + du * b_ref[k : k + 1, :]
        next_ref[k] = state.astype(BF16)
        total = total + state * c_ref[k : k + 1, :]
    gate = gate_ref[...]
    y_ref[...] = (total * (gate / (1.0 + jnp.exp(-gate)))).astype(BF16)


def local(n, snake, hidden, input_conv_weight, input_gate_weight, convolution_taps, convolution_bias,
          step_input_projection, step_norm_gain, step_size_projection, step_size_bias, decay_rates,
          skip, output_weight, adapter_down_maps, adapter_up_maps, tenant, convolution_cache,
          recurrent_cache, incoming_recurrent_states, incoming_conv_states, incoming_buffer_row,
          incoming_slot_index):
    rows, reqs = hidden.shape
    width, chans = input_conv_weight.shape
    rank = step_size_projection.shape[0]
    states = decay_rates.shape[0]
    taps = convolution_cache.shape[0]
    tenants, _, low_rank = adapter_down_maps.shape
    held = incoming_recurrent_states.shape[0]
    m, h = n // 2, n // 4
    share = reqs // n
    sds = jax.ShapeDtypeStruct

    def params(cid):
        return pltpu.CompilerParams(
            collective_id=cid, has_side_effects=True, vmem_limit_bytes=LIMIT)

    conv_rows = -(-held * taps // 16) * 16
    conv_in = incoming_conv_states.reshape(held * taps, n, chans).transpose(1, 0, 2)
    conv_in = jnp.pad(conv_in, ((0, 0), (0, conv_rows - held * taps), (0, 0)))

    x_in, gate_in, land_ssm, land_conv = pl.pallas_call(
        functools.partial(gather_kernel, n, snake),
        name="gather_project",
        out_shape=(sds((chans, reqs), F32), sds((chans, reqs), F32),
                   sds((n, held, states, chans), BF16), sds((n, conv_rows, chans), BF16)),
        in_specs=[VM, ANY, ANY, ANY, ANY],
        out_specs=(VM, VM, ANY, ANY),
        scratch_shapes=[
            pltpu.VMEM((n, rows, reqs), BF16), pltpu.VMEM((width, chans), BF16),
            pltpu.VMEM((width, chans), BF16), DMA((2,)), DMA((3,)),
            DMA((h,)), DMA((h,)), DMA((h,)), DMA((h,)), DMA((m,)), DMA((m,)),
            DMA((n,)), DMA((n,)), DMA((n,)), DMA((n,))],
        compiler_params=params(0),
    )(hidden, input_conv_weight, input_gate_weight, incoming_recurrent_states, conv_in)

    buffers = n * held
    land_ssm = land_ssm.reshape(buffers, states, chans).transpose(1, 0, 2)
    land_conv = land_conv[:, : held * taps].reshape(buffers, taps, chans).transpose(1, 0, 2)
    pick = ((incoming_buffer_row[:, None] == jnp.arange(buffers)[None, :]).astype(F32)).T @ (
        incoming_slot_index[:, None] == jnp.arange(reqs)[None, :]).astype(F32)
    hit = jnp.sum(pick, axis=0, keepdims=True)
    pick = pick.astype(BF16)

    eb = 128
    grid = (chans // eb,)
    whole = lambda *shape: pl.BlockSpec(shape, lambda i: (0,) * len(shape))
    rowb = lambda cols: pl.BlockSpec((eb, cols), lambda i: (i, 0))
    mid = lambda lead, cols: pl.BlockSpec((lead, eb, cols), lambda i: (0, i, 0))
    lastb = lambda lead, m_: pl.BlockSpec((lead, m_, eb), lambda i: (0, 0, i))

    conv_next, u = pl.pallas_call(
        conv_kernel,
        name="conv_step",
        grid=grid,
        out_shape=(sds((taps, chans, reqs), BF16), sds((chans, reqs), BF16)),
        in_specs=[rowb(reqs), mid(taps, reqs), lastb(taps, buffers), whole(buffers, reqs),
                  whole(1, reqs), rowb(taps + 1), rowb(1)],
        out_specs=(mid(taps, reqs), rowb(reqs)),
        compiler_params=pltpu.CompilerParams(vmem_limit_bytes=LIMIT),
    )(x_in, convolution_cache, land_conv, pick, hit, convolution_taps.astype(F32).T,
      convolution_bias.astype(F32)[:, None])

    mix_part = dot0(u, step_input_projection).astype(BF16).reshape(n, share, rank + 2 * states)
    dt_norm, bc = pl.pallas_call(
        functools.partial(mix_kernel, n, rank),
        name="mix_sum",
        out_shape=(sds((n, share, rank), BF16), sds((n, share, 2 * states), F32)),
        in_specs=[VM, VM],
        out_specs=(VM, VM),
        scratch_shapes=[pltpu.VMEM((n, share, rank + 2 * states), BF16)] + [DMA((n,))] * 6,
        compiler_params=params(1),
    )(mix_part, step_norm_gain[None, :])
    dt_norm = dt_norm.reshape(reqs, rank).T
    bc = bc.reshape(reqs, 2 * states).T

    ssm_next, y = pl.pallas_call(
        state_kernel,
        name="state_step",
        grid=grid,
        out_shape=(sds((states, chans, reqs), BF16), sds((chans, reqs), BF16)),
        in_specs=[whole(rank, reqs), pl.BlockSpec((rank, eb), lambda i: (0, i)), rowb(1),
                  rowb(states), rowb(1), rowb(reqs), rowb(reqs), whole(states, reqs),
                  whole(states, reqs), mid(states, reqs), lastb(states, buffers),
                  whole(buffers, reqs), whole(1, reqs)],
        out_specs=(mid(states, reqs), rowb(reqs)),
        compiler_params=pltpu.CompilerParams(vmem_limit_bytes=LIMIT),
    )(dt_norm, step_size_projection, step_size_bias[:, None], decay_rates.T, skip[:, None], u,
      gate_in, bc[:states], bc[states:], recurrent_cache, land_ssm, pick, hit)

    mine = tenant[:, 0][None, :] == jnp.arange(tenants, dtype=jnp.int32)[:, None]
    down = adapter_down_maps.transpose(0, 2, 1).reshape(tenants * low_rank, chans)
    v_all = jnp.dot(down, y, preferred_element_type=F32).reshape(tenants, low_rank, reqs)
    v_part = jnp.sum(jnp.where(mine[:, None, :], v_all, 0.0), axis=0)
    v_part = v_part.T.reshape(n, share, low_rank)

    block = pltpu.VMEM((h, rows, reqs), BF16)
    pairs = pltpu.VMEM((m, rows, reqs), BF16)
    main, v = pl.pallas_call(
        functools.partial(scatter_kernel, n, snake),
        name="project_scatter",
        out_shape=(sds((rows, reqs), F32), sds((n, share, low_rank), BF16)),
        in_specs=[VM, ANY, VM],
        out_specs=(VM, VM),
        scratch_shapes=[
            pltpu.VMEM((chans, width), BF16), pltpu.VMEM((rows, reqs), F32), pairs, pairs,
            block, block, block, block, pltpu.VMEM((n, share, low_rank), F32), DMA((1,)),
            DMA((h,)), DMA((h,)), DMA((h,)), DMA((h,)), DMA((m,)), DMA((m,)),
            DMA((n,)), DMA((n,)), DMA((n,)), DMA((n,))],
        compiler_params=params(2),
    )(y, output_weight, v_part)

    v = v.reshape(reqs, low_rank).T
    v_wide = jnp.where(mine[:, None, :], v[None], jnp.zeros((), BF16))
    up = adapter_up_maps.reshape(tenants * low_rank, rows)
    mixed = main + dot0(up, v_wide.reshape(tenants * low_rank, reqs))
    return mixed.astype(BF16), ssm_next, conv_next


def solution(mesh):
    placed = (
        P("tensor", "group"),
        P(None, "tensor"),
        P(None, "tensor"),
        P(None, "tensor"),
        P("tensor"),
        P("tensor", None),
        P(),
        P(None, "tensor"),
        P("tensor"),
        P(None, "tensor"),
        P("tensor"),
        P("tensor", None),
        P(None, "tensor", None),
        P(None, None, "tensor"),
        P("group", None),
        P(None, "tensor", "group"),
        P(None, "tensor", "group"),
        P(("group", "tensor"), None, None),
        P(("group", "tensor"), None, None),
        P("group"),
        P("group"),
    )
    n = mesh.shape["tensor"]
    snake = mesh.shape["group"] == 2
    return jax.shard_map(
        functools.partial(local, n, snake),
        mesh=mesh,
        in_specs=placed,
        out_specs=(P("tensor", "group"), P(None, "tensor", "group"), P(None, "tensor", "group")),
        check_vma=False,
    )
```

time: 444 us -> 216 us (0.49)
  Pallas kernels: 0 us -> 188 us
  waiting for transfers between devices: 138 us -> 0 us
  local copies, waits for them, and re-layouts: 131 us -> 17.6 us
  blocking collectives: 78.4 us -> 0 us
  matrix products: 40.2 us -> 7.51 us
  other arithmetic: 25.3 us -> 1.88 us
  starting transfers between devices: 14 us -> 0 us
  between operations: 14 us -> 0.78 us
    pallas_call x0 -> x5, Pallas kernels: none -> 188 us  [the longest x1 71.5 us: local(): pl.pallas_call(functools.partial(gather_kernel, n, snake), name='gather_p...]
    unnamed x47 -> x26, local copies, waits for them, and re-layouts: 87.6 us -> 1.98 us
    psum x1 -> x0, blocking collectives: 78.4 us -> none  [local(): value_lowrank = lax.psum(value_portion, 'tensor').astype(jnp.bfloat16)]
    reduce_scatter x1 -> x0, waiting for transfers between devices: 64.6 us -> none  [local(): lax.psum_scatter(lax.dot_general(output_weight, y_low, CONTRACT, preferre...]
    psum x1 -> x0, waiting for transfers between devices: 51.7 us -> none  [local(): mixing = lax.psum(partial_mix, 'tensor')]
    dot_general x7 -> x4, matrix products: 40.2 us -> 7.51 us  [the longest x2 4.26 us: dot0(): return lax.dot_general(a, b, CONTRACT, preferred_element_type=F32)]
    all_gather x1 -> x0, waiting for transfers between devices: 21 us -> none  [local(): piece = lax.all_gather(hidden, 'tensor', axis=0, tiled=True)]
    all_to_all x2 -> x0, local copies, waits for them, and re-layouts: 20 us -> none  [the longest x1 10.3 us: local(): lax.all_to_all(incoming_recurrent_states, 'tensor', split_axis=2, concat_...]
  transfers between devices with their start and end apart: 5 -> 0, of which waited for: 3 -> 0; matrix products, arithmetic and copies ran while one was open for 36% -> 0% of each run, Pallas kernels for 0% -> 0%
where the time goes in v1:
time: 216 us
  Pallas kernels  188 us (87%)
  local copies, waits for them, and re-layouts  17.6 us (8%)
  matrix products  7.51 us (3%)
    pallas_call x1, Pallas kernels, local(): pl.pallas_call(functools.partial(gather_kernel, n, snake), name='gather_p...  71.5 us
    pallas_call x1, Pallas kernels, local(): pl.pallas_call(functools.partial(scatter_kernel, n, snake), name='project...  65.9 us
    pallas_call x1, Pallas kernels, local(): pl.pallas_call(functools.partial(mix_kernel, n, rank), name='mix_sum', ou...  32.7 us
    pallas_call x1, Pallas kernels, local(): pl.pallas_call(state_kernel, name='state_step', grid=grid, out_shape=(sds...  13.2 us
    pallas_call x1, Pallas kernels, local(): pl.pallas_call(conv_kernel, name='conv_step', grid=grid, out_shape=(sds((...  4.66 us

profile of v1, /device:TPU:0, one launch (start us, length us, event | category | flops | bytes accessed | tf_op | source)
XLA Modules:
  0.0 215.7 jit_solution(13053768597251525521)
XLA Ops:
  0.6 0.0 copy-start
  0.6 1.1 copy.48
  1.7 0.1 reshape.61
  1.9 0.1 copy.72
  1.9 0.7 pad.4.conv_hbm
  2.7 71.5 %gather_project.1 = (f32[512,512]{1,0:T(8,128)}, f32[512,512]{1,0:T(8,128)}, bf16[16,2,16,512]{3,2,1,0:T(8,128)(2,1)}, bf16[16,16,512]{2,1,0:T(8,128)(2,1)}) custom-call(bf16[512,512]{1,0:T(8,128)(2,1)} %h_ref.1, bf16[8192,512]{1,0:T(8,128)(2,1)} %wx_hbm.1, bf16[8192,512]{1,0:T(8,128)(2,1)} %wg_hbm.1, bf16[2,16,8192]{2,1,0:T(8,128)(2,1)} %ssm_hbm.1, ...), custom_call_target="tpu_custom_call" | custom-call | tf_op jit(solution)/shard_map/gather_project/pallas_call | solution.py:411
  74.2 0.9 slice.9
  75.2 0.1 reshape.62
  75.2 0.7 copy.73
  75.9 1.4 fusion.11
  77.4 0.9 copy.52.bias_ref
  78.2 0.9 copy.51
  79.1 4.7 %conv_step.1 = (bf16[3,512,512]{2,1,0:T(8,128)(2,1)}, bf16[512,512]{1,0:T(8,128)(2,1)}) custom-call(f32[512,512]{1,0:T(8,128)} %get-tuple-element.15.x_ref, bf16[3,512,512]{2,1,0:T(8,128)(2,1)} %cache_ref.2, bf16[3,32,512]{2,1,0:T(8,128)(2,1)} %bitcast.59, bf16[32,512]{1,0:T(8,128)(2,1)} %get-tuple-element.30.pick_ref, f32[1,512]{1,0:T(1,128)} %bitcast.64, ...), custom_call_target="tpu_custom_call" | custom-call | tf_op jit(solution)/shard_map/conv_step/pallas_call | solution.py:441
  83.8 1.5 convolution_convert_fusion
  85.3 1.1 copy.53
  86.4 32.7 %mix_sum.1 = (bf16[16,32,512]{2,1,0:T(8,128)(2,1)}, f32[16,32,32]{2,1,0:T(8,128)}) custom-call(bf16[16,32,544]{2,1,0:T(8,128)(2,1)} %bitcast.49, f32[1,512]{1,0:T(1,128)} %bitcast.66), custom_call_target="tpu_custom_call" | custom-call | tf_op jit(solution)/shard_map/mix_sum/pallas_call | solution.py:454
  119.1 1.1 copy.65
  120.1 0.6 fusion.10
  120.7 2.1 copy.54
  122.8 1.1 copy.71
  123.9 0.9 copy.55
  124.8 0.9 copy.58.bias_ref
  125.6 0.9 copy.59.skip_ref
  126.5 13.2 %state_step.1 = (bf16[16,512,512]{2,1,0:T(8,128)(2,1)}, bf16[512,512]{1,0:T(8,128)(2,1)}) custom-call(bf16[512,512]{1,0:T(8,128)(2,1)} %bitcast.50, bf16[512,512]{1,0:T(8,128)(2,1)} %proj_ref.1, f32[512,1]{1,0:T(8,128)} %copy.58.bias_ref, f32[512,16]{1,0:T(8,128)} %bitcast.52, f32[512,1]{1,0:T(8,128)} %copy.59.skip_ref, ...), custom_call_target="tpu_custom_call" | custom-call | tf_op jit(solution)/shard_map/state_step/pallas_call | solution.py:466
  139.7 1.8 convolution_bitcast_fusion
  141.5 0.0 copy-start.7
  141.5 1.8 copy.60
  143.4 1.9 select_reduce_fusion
  145.2 0.8 copy.61
  146.1 65.9 %project_scatter.1 = (f32[512,512]{1,0:T(8,128)}, bf16[16,32,64]{2,1,0:T(8,128)(2,1)}) custom-call(bf16[512,512]{1,0:T(8,128)(2,1)} %get-tuple-element.22.y_ref, bf16[512,8192]{1,0:T(8,128)(2,1)} %w_hbm.1, f32[16,32,64]{2,1,0:T(8,128)} %bitcast.53), custom_call_target="tpu_custom_call" | custom-call | tf_op jit(solution)/shard_map/project_scatter/pallas_call | solution.py:488
  212.0 1.0 copy.62
  213.0 2.8 %fusion.1 = bf16[512,512]{1,0:T(8,128)(2,1)} fusion(f32[512,512]{1,0:T(8,128)} %get-tuple-element.23, bf16[16,64,512]{2,1,0:T(8,128)(2,1)S(1)} %copy-done.9, pred[16,512]{1,0:T(8,128)(4,1)S(1)} %iota_compare_fusion.2, bf16[64,512]{1,0:T(8,128)(2,1)S(1)} %copy.62), kind=kOutput, calls=%fused_computation.5 | convolution fusion | flops 537919488 | bytes 2695168 | tf_op jit(solution)/shard_map/dot_general | solution.py:20
  (24 shorter events, 0.1 us)
Async XLA Ops:
  0.6 139.0 %copy-start = (bf16[16,512,64]{1,2,0:T(8,128)(2,1)S(1)}, bf16[16,512,64]{1,2,0:T(8,128)(2,1)}, u32[]{:S(2)}) copy-start(bf16[16,512,64]{1,2,0:T(8,128)(2,1)} %param.33) | copy-start | bytes 3145732
  2.7 73.2 %copy-start.10 = (s32[32]{0:T(128)S(1)}, s32[32]{0:T(128)}, u32[]{:S(2)}) copy-start(s32[32]{0:T(128)} %param.41) | copy-start | bytes 388
  2.7 73.2 %copy-start.11 = (s32[32]{0:T(128)S(1)}, s32[32]{0:T(128)}, u32[]{:S(2)}) copy-start(s32[32]{0:T(128)} %param.40) | copy-start | bytes 388
  2.7 74.7 %copy-start.8 = (bf16[512]{0:T(512)(128)(2,1)S(1)}, bf16[512]{0:T(512)(128)(2,1)}, u32[]{:S(2)}) copy-start(bf16[512]{0:T(512)(128)(2,1)} %param.25) | copy-start | bytes 3076
  2.7 75.6 %copy-start.4 = (bf16[4,512]{1,0:T(4,128)(2,1)S(1)}, bf16[4,512]{1,0:T(4,128)(2,1)}, u32[]{:S(2)}) copy-start(bf16[4,512]{1,0:T(4,128)(2,1)} %param.24) | copy-start | bytes 12292
  75.2 8.5 %copy-start.1 = (bf16[512,544]{0,1:T(8,128)(2,1)S(1)}, bf16[512,544]{0,1:T(8,128)(2,1)}, u32[]{:S(2)}) copy-start(bf16[512,544]{0,1:T(8,128)(2,1)} %param.26) | copy-start | bytes 1671172
  85.3 37.6 %copy-start.2 = (bf16[16,2,16,512]{3,2,1,0:T(8,128)(2,1)S(1)}, bf16[16,2,16,512]{3,2,1,0:T(8,128)(2,1)}, u32[]{:S(2)}) copy-start(bf16[16,2,16,512]{3,2,1,0:T(8,128)(2,1)} %get-tuple-element.21) | copy-start | bytes 1572868
  85.3 38.6 %copy-start.3 = (f32[16,512]{1,0:T(8,128)S(1)}, f32[16,512]{1,0:T(8,128)}, u32[]{:S(2)}) copy-start(f32[16,512]{1,0:T(8,128)} %param.30) | copy-start | bytes 98308
  85.3 39.5 %copy-start.5 = (f32[512]{0:T(512)S(1)}, f32[512]{0:T(512)}, u32[]{:S(2)}) copy-start(f32[512]{0:T(512)} %param.29) | copy-start | bytes 6148
  86.4 39.3 %copy-start.6 = (f32[512]{0:T(512)S(1)}, f32[512]{0:T(512)}, u32[]{:S(2)}) copy-start(f32[512]{0:T(512)} %param.31) | copy-start | bytes 6148
  141.5 1.9 copy-start.7
  146.1 66.9 %copy-start.9 = (bf16[16,64,512]{2,1,0:T(8,128)(2,1)S(1)}, bf16[16,64,512]{2,1,0:T(8,128)(2,1)}, u32[]{:S(2)}) copy-start(bf16[16,64,512]{2,1,0:T(8,128)(2,1)} %param.34) | copy-start | bytes 3145732

commit v2 on v1

--- a/solution.py
+++ b/solution.py
@@ -203,41 +203,78 @@
         remote(conv_out.at[t], conv_out.at[t], cs.at[d], cr.at[d], t).wait_recv()
 
 
-def mix_kernel(n, rank, part_ref, gain_ref, dt_ref, bc_ref, recv, s1, r1, s2, r2, s3, r3):
+def mix_kernel(n, rank, part_ref, gain_ref, out_ref, pair, recv, s0, r0, s1, r1, s2, r2, s3, r3):
     me = lax.axis_index("tensor")
-    greet_all(me, n)
-
-    @pl.loop(1, n)
-    def _(d):
-        t = lax.rem(me + d, n)
-        remote(part_ref.at[t], recv.at[d], s1.at[d], r1.at[d], t).start()
-
-    recv[0] = part_ref[me]
-
-    @pl.loop(1, n)
-    def _(d):
-        remote(part_ref.at[0], recv.at[d], s1.at[d], r1.at[d], lax.rem(me + d, n)).wait()
-
-    total = jnp.sum(recv[...].astype(F32), axis=0)
+    m = n // 2
+    core = lax.rem(me, 2)
+    chip = me // 2
+    sibling = me + 1 - 2 * core
+
+    def peer(d):
+        return lax.rem(chip + d, m) * 2 + core
+
+    barrier = pltpu.get_barrier_semaphore()
+    pl.semaphore_signal(barrier, inc=1, device_id={"tensor": sibling},
+                        device_id_type=pl.DeviceIdType.MESH)
+
+    @pl.loop(1, m)
+    def _(d):
+        pl.semaphore_signal(barrier, inc=1, device_id={"tensor": peer(d)},
+                            device_id_type=pl.DeviceIdType.MESH)
+
+    pl.semaphore_wait(barrier, m)
+
+    swap = remote(part_ref.at[:, 1 - core], pair, s0.at[0], r0.at[0], sibling)
+    swap.start()
+    swap.wait()
+
+    @pl.loop(0, m)
+    def _(d):
+        q = lax.rem(chip + d, m)
+        recv[d] = (part_ref[q, core].astype(F32) + pair[q].astype(F32)).astype(BF16)
+
+    @pl.loop(1, m)
+    def _(d):
+        remote(recv.at[d], recv.at[m + d], s1.at[d], r1.at[d], peer(d)).start()
+
+    @pl.loop(1, m)
+    def _(d):
+        remote(recv.at[d], recv.at[m + d], s1.at[d], r1.at[d], peer(d)).wait()
+
+    total = recv[0].astype(F32) + jnp.sum(recv[pl.ds(m + 1, m - 1)].astype(F32), axis=0)
     dt = total[:, :rank]
     factor = lax.rsqrt(jnp.mean(dt * dt, axis=1, keepdims=True) + 1e-06)
-    dt_ref[me] = (dt * factor * gain_ref[...]).astype(BF16)
-    bc_ref[me] = total[:, rank:]
-
-    @pl.loop(1, n)
-    def _(d):
-        t = lax.rem(me + d, n)
-        remote(dt_ref.at[me], dt_ref.at[me], s2.at[d], r2.at[d], t).start()
-        remote(bc_ref.at[me], bc_ref.at[me], s3.at[d], r3.at[d], t).start()
-
-    @pl.loop(1, n)
-    def _(d):
-        t = lax.rem(me + n - d, n)
-        remote(dt_ref.at[t], dt_ref.at[t], s2.at[d], r2.at[d], t).wait()
-        remote(bc_ref.at[t], bc_ref.at[t], s3.at[d], r3.at[d], t).wait()
-
-
-def scatter_kernel(n, snake, y_ref, w_hbm, v_ref, out_ref, v_out, w, acc, sbuf, rbuf, rsend, rrecv,
+    out_ref[me, :, pl.ds(0, rank)] = (dt * factor * gain_ref[...]).astype(BF16)
+    out_ref[me, :, pl.ds(rank, total.shape[1] - rank)] = total[:, rank:].astype(BF16)
+
+    def forward(d, t):
+        return remote(out_ref.at[t], out_ref.at[t], s3.at[d], r3.at[d], sibling)
+
+    @pl.loop(1, m)
+    def _(d):
+        remote(out_ref.at[me], out_ref.at[me], s2.at[d], r2.at[d], peer(d)).start()
+
+    forward(0, me).start()
+
+    @pl.loop(1, m)
+    def _(d):
+        t = peer(m - d)
+        remote(out_ref.at[t], out_ref.at[t], s2.at[d], r2.at[d], t).wait_recv()
+        forward(d, t).start()
+
+    @pl.loop(0, m)
+    def _(d):
+        t = peer(m - d)
+        forward(d, t).wait_send()
+        forward(d, t + 1 - 2 * core).wait_recv()
+
+    @pl.loop(1, m)
+    def _(d):
+        remote(out_ref.at[me], out_ref.at[me], s2.at[d], r2.at[d], peer(d)).wait_send()
+
+
+def scatter_kernel(n, snake, y_ref, w_hbm, down_ref, up_ref, tenant_ref, out_ref, w, acc, more, v_ref,
+                   v_out, sbuf, rbuf, rsend, rrecv,
                    lsend, lrecv, vrecv, wsem, rs, rr, ls, lr, ss, sr, s1, r1, s2, r2):
     ring = Ring(n, snake)
     me, m, h = ring.me, ring.m, ring.m // 2
@@ -250,12 +287,6 @@
     right, left = ring.at(1), ring.at(-1)
     other = 1 - ring.core
 
-    @pl.loop(1, n)
-    def _(d):
-        t = lax.rem(me + d, n)
-        remote(v_ref.at[t], vrecv.at[d], s1.at[d], r1.at[d], t).start()
-
-    vrecv[0] = v_ref[me]
     cw.wait()
 
     def part(t):
@@ -289,6 +320,26 @@
     start_half(True).start()
     lsend[0, second] = acc[second].astype(BF16)
     start_half(False).start()
+
+    _, share, low = v_ref.shape
+    batch = 4 * low
+    count = down_ref.shape[0] // batch
+
+    def down(i, total):
+        every = jnp.dot(down_ref[pl.ds(pl.multiple_of(i * batch, batch), batch), :], y_ref[...],
+                        preferred_element_type=F32)
+        for j in range(4):
+            total = total + jnp.where(tenant_ref[...] == 4 * i + j, every[j * low : (j + 1) * low], 0.0)
+        return total
+
+    v_mine = lax.fori_loop(0, count, down, jnp.zeros((low, y_ref.shape[1]), F32))
+    v_ref[...] = v_mine.T.reshape(n, share, low)
+    vrecv[0] = v_ref[me]
+
+    @pl.loop(1, n)
+    def _(d):
+        t = lax.rem(me + d, n)
+        remote(v_ref.at[t], vrecv.at[d], s1.at[d], r1.at[d], t).start()
 
     give(1, h - 1)
     give(2, 1 - h)
@@ -327,10 +378,26 @@
         going(s, False).start()
 
     give(m - 1, 0)
+
+    @pl.loop(1, n)
+    def _(d):
+        t = lax.rem(me + n - d, n)
+        remote(v_out.at[t], v_out.at[t], s2.at[d], r2.at[d], t).wait()
+
+    v_all = v_out[...].astype(F32).reshape(n * share, low).T
+    more[...] = jnp.zeros_like(more)
+
+    @pl.loop(0, count)
+    def _(i):
+        wide = jnp.concatenate(
+            [jnp.where(tenant_ref[...] == 4 * i + j, v_all, 0.0) for j in range(4)], axis=0)
+        more[...] += dot0(up_ref[pl.ds(pl.multiple_of(i * batch, batch), batch), :], wide.astype(BF16))
+
     take(m - 1, 0)
+    more[...] += acc[...]
     going(h - 1, True).wait_recv()
     going(h - 1, False).wait_recv()
-    out_ref[...] = acc[...] + rrecv[h - 1].astype(F32) + lrecv[h - 1].astype(F32)
+    out_ref[...] = (more[...] + rrecv[h - 1].astype(F32) + lrecv[h - 1].astype(F32)).astype(BF16)
 
     start_half(True).wait_send()
     start_half(False).wait_send()
@@ -343,11 +410,6 @@
     @pl.loop(0, m)
     def _(k):
         sib(k).wait_send()
-
-    @pl.loop(1, n)
-    def _(d):
-        t = lax.rem(me + n - d, n)
-        remote(v_out.at[t], v_out.at[t], s2.at[d], r2.at[d], t).wait()
 
 
 def conv_kernel(x_ref, cache_ref, land_ref, pick_ref, hit_ref, taps_ref, bias_ref, next_ref, u_ref):
@@ -366,9 +428,12 @@
     u_ref[...] = (total / (1.0 + jnp.exp(-total))).astype(BF16)
 
 
-def state_kernel(dt_ref, proj_ref, bias_ref, decay_ref, skip_ref, u_ref, gate_ref, b_ref, c_ref,
+def state_kernel(dt_ref, proj_ref, bias_ref, decay_ref, skip_ref, u_ref, gate_ref,
                  cache_ref, land_ref, pick_ref, hit_ref, next_ref, y_ref):
-    pre = dot0(proj_ref[...], dt_ref[...]) + bias_ref[...]
+    rank, states = proj_ref.shape[0], cache_ref.shape[0]
+    pre = dot0(proj_ref[...], dt_ref[pl.ds(0, rank), :]) + bias_ref[...]
+    b_in = dt_ref[pl.ds(rank, states), :].astype(F32)
+    c_out = dt_ref[pl.ds(rank + states, states), :].astype(F32)
     delta = jnp.maximum(pre, 0.0) + jnp.log1p(jnp.exp(-jnp.abs(pre)))
     u = u_ref[...].astype(F32)
     du = delta * u
@@ -377,9 +442,9 @@
     for k in range(cache_ref.shape[0]):
         placed = dot0(land_ref[k], pick_ref[...])
         old = jnp.where(hit, placed, cache_ref[k].astype(F32))
-        state = jnp.exp(-delta * decay_ref[:, k : k + 1]) * old + du * b_ref[k : k + 1, :]
+        state = jnp.exp(-delta * decay_ref[:, k : k + 1]) * old + du * b_in[k : k + 1, :]
         next_ref[k] = state.astype(BF16)
-        total = total + state * c_ref[k : k + 1, :]
+        total = total + state * c_out[k : k + 1, :]
     gate = gate_ref[...]
     y_ref[...] = (total * (gate / (1.0 + jnp.exp(-gate)))).astype(BF16)
 
@@ -450,60 +515,53 @@
     )(x_in, convolution_cache, land_conv, pick, hit, convolution_taps.astype(F32).T,
       convolution_bias.astype(F32)[:, None])
 
-    mix_part = dot0(u, step_input_projection).astype(BF16).reshape(n, share, rank + 2 * states)
-    dt_norm, bc = pl.pallas_call(
+    outs = rank + 2 * states
+    mix_part = dot0(u, step_input_projection).astype(BF16).reshape(m, 2, share, outs)
+    mixed_in = pl.pallas_call(
         functools.partial(mix_kernel, n, rank),
         name="mix_sum",
-        out_shape=(sds((n, share, rank), BF16), sds((n, share, 2 * states), F32)),
+        out_shape=sds((n, share, outs), BF16),
         in_specs=[VM, VM],
-        out_specs=(VM, VM),
-        scratch_shapes=[pltpu.VMEM((n, share, rank + 2 * states), BF16)] + [DMA((n,))] * 6,
+        out_specs=VM,
+        scratch_shapes=[pltpu.VMEM((m, share, outs), BF16), pltpu.VMEM((n, share, outs), BF16),
+                        DMA((1,)), DMA((1,))] + [DMA((m,))] * 6,
         compiler_params=params(1),
     )(mix_part, step_norm_gain[None, :])
-    dt_norm = dt_norm.reshape(reqs, rank).T
-    bc = bc.reshape(reqs, 2 * states).T
+    mixed_in = mixed_in.reshape(reqs, outs).T
 
     ssm_next, y = pl.pallas_call(
         state_kernel,
         name="state_step",
         grid=grid,
         out_shape=(sds((states, chans, reqs), BF16), sds((chans, reqs), BF16)),
-        in_specs=[whole(rank, reqs), pl.BlockSpec((rank, eb), lambda i: (0, i)), rowb(1),
-                  rowb(states), rowb(1), rowb(reqs), rowb(reqs), whole(states, reqs),
-                  whole(states, reqs), mid(states, reqs), lastb(states, buffers),
+        in_specs=[whole(outs, reqs), pl.BlockSpec((rank, eb), lambda i: (0, i)), rowb(1),
+                  rowb(states), rowb(1), rowb(reqs), rowb(reqs), mid(states, reqs), lastb(states, buffers),
                   whole(buffers, reqs), whole(1, reqs)],
         out_specs=(mid(states, reqs), rowb(reqs)),
         compiler_params=pltpu.CompilerParams(vmem_limit_bytes=LIMIT),
-    )(dt_norm, step_size_projection, step_size_bias[:, None], decay_rates.T, skip[:, None], u,
-      gate_in, bc[:states], bc[states:], recurrent_cache, land_ssm, pick, hit)
-
-    mine = tenant[:, 0][None, :] == jnp.arange(tenants, dtype=jnp.int32)[:, None]
+    )(mixed_in, step_size_projection, step_size_bias[:, None], decay_rates.T, skip[:, None], u,
+      gate_in, recurrent_cache, land_ssm, pick, hit)
+
     down = adapter_down_maps.transpose(0, 2, 1).reshape(tenants * low_rank, chans)
-    v_all = jnp.dot(down, y, preferred_element_type=F32).reshape(tenants, low_rank, reqs)
-    v_part = jnp.sum(jnp.where(mine[:, None, :], v_all, 0.0), axis=0)
-    v_part = v_part.T.reshape(n, share, low_rank)
-
+    up = adapter_up_maps.reshape(tenants * low_rank, rows)
     block = pltpu.VMEM((h, rows, reqs), BF16)
     pairs = pltpu.VMEM((m, rows, reqs), BF16)
-    main, v = pl.pallas_call(
+    mixed = pl.pallas_call(
         functools.partial(scatter_kernel, n, snake),
         name="project_scatter",
-        out_shape=(sds((rows, reqs), F32), sds((n, share, low_rank), BF16)),
-        in_specs=[VM, ANY, VM],
-        out_specs=(VM, VM),
+        out_shape=sds((rows, reqs), BF16),
+        in_specs=[VM, ANY, VM, VM, VM],
+        out_specs=VM,
         scratch_shapes=[
-            pltpu.VMEM((chans, width), BF16), pltpu.VMEM((rows, reqs), F32), pairs, pairs,
+            pltpu.VMEM((chans, width), BF16), pltpu.VMEM((rows, reqs), F32),
+            pltpu.VMEM((rows, reqs), F32), pltpu.VMEM((n, share, low_rank), F32),
+            pltpu.VMEM((n, share, low_rank), BF16), pairs, pairs,
             block, block, block, block, pltpu.VMEM((n, share, low_rank), F32), DMA((1,)),
             DMA((h,)), DMA((h,)), DMA((h,)), DMA((h,)), DMA((m,)), DMA((m,)),
             DMA((n,)), DMA((n,)), DMA((n,)), DMA((n,))],
         compiler_params=params(2),
-    )(y, output_weight, v_part)
-
-    v = v.reshape(reqs, low_rank).T
-    v_wide = jnp.where(mine[:, None, :], v[None], jnp.zeros((), BF16))
-    up = adapter_up_maps.reshape(tenants * low_rank, rows)
-    mixed = main + dot0(up, v_wide.reshape(tenants * low_rank, reqs))
-    return mixed.astype(BF16), ssm_next, conv_next
+    )(y, output_weight, down, up, tenant.reshape(1, reqs))
+    return mixed, ssm_next, conv_next
 
 
 def solution(mesh):

time: 216 us -> 197 us (0.912)
  Pallas kernels: 188 us -> 173 us
  matrix products: 7.51 us -> 3.6 us
    pallas_call x1, Pallas kernels: 32.7 us -> 22.7 us  [local(): pl.pallas_call(functools.partial(mix_kernel, n, rank), name='mix_sum', ou...]
    pallas_call x1, Pallas kernels: 65.9 us -> 61.4 us  [local(): pl.pallas_call(functools.partial(scatter_kernel, n, snake), name='project...]
    dot_general x2 -> x1, matrix products: 4.26 us -> 1.49 us  [dot0(): return lax.dot_general(a, b, CONTRACT, preferred_element_type=F32)]
    unnamed x26 -> x5, local copies, waits for them, and re-layouts: 1.98 us -> 4.44 us
where the time goes in v2:
time: 197 us; the launch traced here: 196 us
  Pallas kernels  173 us (88%)
  local copies, waits for them, and re-layouts  17.8 us (9%)
  matrix products  3.6 us (2%)
    pallas_call x1, Pallas kernels, local(): pl.pallas_call(functools.partial(gather_kernel, n, snake), name='gather_p...  71.5 us
    pallas_call x1, Pallas kernels, local(): pl.pallas_call(functools.partial(scatter_kernel, n, snake), name='project...  61.4 us
    pallas_call x1, Pallas kernels, local(): pl.pallas_call(functools.partial(mix_kernel, n, rank), name='mix_sum', ou...  22.7 us
    pallas_call x1, Pallas kernels, local(): pl.pallas_call(state_kernel, name='state_step', grid=grid, out_shape=(sds...  13.2 us
    pallas_call x1, Pallas kernels, local(): pl.pallas_call(conv_kernel, name='conv_step', grid=grid, out_shape=(sds((...  4.66 us
    unnamed x5, local copies, waits for them, and re-layouts  4.44 us

profile of v2, /device:TPU:0, one launch (start us, length us, event | category | flops | bytes accessed | tf_op | source)
XLA Modules:
  0.0 196.2 jit_solution(2194452092814004435)
XLA Ops:
  0.6 0.0 copy-start
  0.6 0.7 broadcast_in_dim.27
  1.4 2.1 %fusion.3 = (f32[512]{0:T(512)}, bf16[32,512]{1,0:T(8,128)(2,1)}) fusion(s32[32]{0:T(128)} %param.41, s32[32]{0:T(128)} %param.40), kind=kOutput, calls=%fused_computation.9 | convolution fusion | flops 1098240 | bytes 35072 | tf_op jit(solution)/shard_map/dot_general | solution.py:494
  3.5 1.0 copy.29
  4.5 0.1 reshape.32
  4.6 0.1 copy.45
  4.7 0.7 pad.4.conv_hbm
  5.4 0.8 copy.33.bias_ref
  6.3 1.5 copy.32
  7.8 1.5 copy.38.bias_ref
  9.4 1.6 copy.36
  10.9 1.5 copy.39.skip_ref
  12.5 71.5 %gather_project.1 = (f32[512,512]{1,0:T(8,128)}, f32[512,512]{1,0:T(8,128)}, bf16[16,2,16,512]{3,2,1,0:T(8,128)(2,1)}, bf16[16,16,512]{2,1,0:T(8,128)(2,1)}) custom-call(bf16[512,512]{1,0:T(8,128)(2,1)} %h_ref.1, bf16[8192,512]{1,0:T(8,128)(2,1)} %wx_hbm.1, bf16[8192,512]{1,0:T(8,128)(2,1)} %wg_hbm.1, bf16[2,16,8192]{2,1,0:T(8,128)(2,1)} %ssm_hbm.1, ...), custom_call_target="tpu_custom_call" | custom-call | tf_op jit(solution)/shard_map/gather_project/pallas_call | solution.py:476
  84.0 0.9 slice.3
  84.9 0.1 reshape.33
  85.0 0.7 copy.46
  85.6 4.7 %conv_step.1 = (bf16[3,512,512]{2,1,0:T(8,128)(2,1)}, bf16[512,512]{1,0:T(8,128)(2,1)}) custom-call(f32[512,512]{1,0:T(8,128)} %get-tuple-element.11.x_ref, bf16[3,512,512]{2,1,0:T(8,128)(2,1)} %cache_ref.2, bf16[3,32,512]{2,1,0:T(8,128)(2,1)} %bitcast.37, bf16[32,512]{1,0:T(8,128)(2,1)} %get-tuple-element.20.pick_ref, f32[1,512]{1,0:T(1,128)} %bitcast.39, ...), custom_call_target="tpu_custom_call" | custom-call | tf_op jit(solution)/shard_map/conv_step/pallas_call | solution.py:506
  90.3 2.2 %copy.44 = bf16[32,16,512]{2,0,1:T(8,128)(2,1)} copy(bf16[32,16,512]{2,1,0:T(8,128)(2,1)} %bitcast.36) | data formatting | bytes 1048576 | tf_op jit(solution)/shard_map/reshape | solution.py:492
  92.4 0.0 copy-done
  92.4 1.5 convolution_convert_fusion
  93.9 1.1 copy.34
  95.0 22.7 %mix_sum.1 = bf16[16,32,544]{2,1,0:T(8,128)(2,1)} custom-call(bf16[8,2,32,544]{3,2,1,0:T(8,128)(2,1)} %bitcast.27, f32[1,512]{1,0:T(1,128)} %bitcast.43), custom_call_target="tpu_custom_call" | custom-call | tf_op jit(solution)/shard_map/mix_sum/pallas_call | solution.py:520
  117.7 2.1 %copy.35 = bf16[512,544]{0,1:T(8,128)(2,1)} copy(bf16[512,544]{1,0:T(8,128)(2,1)} %bitcast.28) | data formatting | bytes 1114112 | tf_op jit(solution)/shard_map/reshape | solution.py:530
  119.8 13.2 %state_step.1 = (bf16[16,512,512]{2,1,0:T(8,128)(2,1)}, bf16[512,512]{1,0:T(8,128)(2,1)}) custom-call(bf16[544,512]{1,0:T(8,128)(2,1)} %bitcast.29, bf16[512,512]{1,0:T(8,128)(2,1)} %proj_ref.1, f32[512,1]{1,0:T(8,128)} %copy.38.bias_ref, f32[512,16]{1,0:T(8,128)} %bitcast.33, f32[512,1]{1,0:T(8,128)} %copy.39.skip_ref, ...), custom_call_target="tpu_custom_call" | custom-call | tf_op jit(solution)/shard_map/state_step/pallas_call | solution.py:532
  133.0 61.4 %project_scatter.1 = bf16[512,512]{1,0:T(8,128)(2,1)} custom-call(bf16[512,512]{1,0:T(8,128)(2,1)} %get-tuple-element.16.y_ref, bf16[512,8192]{1,0:T(8,128)(2,1)} %w_hbm.1, bf16[1024,512]{1,0:T(8,128)(2,1)} %bitcast.31, bf16[1024,512]{1,0:T(8,128)(2,1)} %bitcast.32, s32[1,512]{1,0:T(1,128)} %bitcast.44), custom_call_target="tpu_custom_call" | custom-call | tf_op jit(solution)/shard_map/project_scatter/pallas_call | solution.py:549
  194.4 1.9 copy.48
Async XLA Ops:
  0.6 91.8 %copy-start = (bf16[512,544]{0,1:T(8,128)(2,1)S(1)}, bf16[512,544]{0,1:T(8,128)(2,1)}, u32[]{:S(2)}) copy-start(bf16[512,544]{0,1:T(8,128)(2,1)} %param.26) | copy-start | bytes 1671172

commit v3 on v2

--- a/solution.py
+++ b/solution.py
@@ -148,14 +148,10 @@
     def step(s, last):
         a, b = ring.at(-1 - s), ring.at(1 + s)
         remote(gath.at[a], gath.at[a], rs.at[s], rr.at[s], right).wait_recv()
+        (right_half() if last else to_right(s + 1)).start()
+        to_sibling(1 + 2 * s, a).start()
         remote(gath.at[b], gath.at[b], ls.at[s], lr.at[s], left).wait_recv()
-        if last:
-            right_half().start()
-            left_half().start()
-        else:
-            to_right(s + 1).start()
-            to_left(s + 1).start()
-        to_sibling(1 + 2 * s, a).start()
+        (left_half() if last else to_left(s + 1)).start()
         to_sibling(2 + 2 * s, b).start()
         compute(a)
         compute(b)
@@ -412,37 +408,39 @@
         sib(k).wait_send()
 
 
-def conv_kernel(x_ref, cache_ref, land_ref, pick_ref, hit_ref, taps_ref, bias_ref, next_ref, u_ref):
+def conv_kernel(x_ref, cache_ref, land_ref, pick_ref, hit_ref, chan_ref, next_ref, u_ref):
     hit = hit_ref[...] > 0
-    total = bias_ref[...]
     count = cache_ref.shape[0]
+    chan = chan_ref[...].T
+    total = chan[:, count + 1 : count + 2]
     for k in range(count):
         placed = dot0(land_ref[k], pick_ref[...])
         old = jnp.where(hit, placed, cache_ref[k].astype(F32))
-        total = total + old * taps_ref[:, k : k + 1]
+        total = total + old * chan[:, k : k + 1]
         if k > 0:
             next_ref[k - 1] = old.astype(BF16)
     low = x_ref[...].astype(BF16)
     next_ref[count - 1] = low
-    total = total + low.astype(F32) * taps_ref[:, count : count + 1]
+    total = total + low.astype(F32) * chan[:, count : count + 1]
     u_ref[...] = (total / (1.0 + jnp.exp(-total))).astype(BF16)
 
 
-def state_kernel(dt_ref, proj_ref, bias_ref, decay_ref, skip_ref, u_ref, gate_ref,
+def state_kernel(dt_ref, proj_ref, chan_ref, u_ref, gate_ref,
                  cache_ref, land_ref, pick_ref, hit_ref, next_ref, y_ref):
     rank, states = proj_ref.shape[0], cache_ref.shape[0]
-    pre = dot0(proj_ref[...], dt_ref[pl.ds(0, rank), :]) + bias_ref[...]
+    chan = chan_ref[...].T
+    pre = dot0(proj_ref[...], dt_ref[pl.ds(0, rank), :]) + chan[:, states : states + 1]
     b_in = dt_ref[pl.ds(rank, states), :].astype(F32)
     c_out = dt_ref[pl.ds(rank + states, states), :].astype(F32)
     delta = jnp.maximum(pre, 0.0) + jnp.log1p(jnp.exp(-jnp.abs(pre)))
     u = u_ref[...].astype(F32)
     du = delta * u
     hit = hit_ref[...] > 0
-    total = skip_ref[...] * u
+    total = chan[:, states + 1 : states + 2] * u
     for k in range(cache_ref.shape[0]):
         placed = dot0(land_ref[k], pick_ref[...])
         old = jnp.where(hit, placed, cache_ref[k].astype(F32))
-        state = jnp.exp(-delta * decay_ref[:, k : k + 1]) * old + du * b_in[k : k + 1, :]
+        state = jnp.exp(-delta * chan[:, k : k + 1]) * old + du * b_in[k : k + 1, :]
         next_ref[k] = state.astype(BF16)
         total = total + state * c_out[k : k + 1, :]
     gate = gate_ref[...]
@@ -503,17 +501,23 @@
     mid = lambda lead, cols: pl.BlockSpec((lead, eb, cols), lambda i: (0, i, 0))
     lastb = lambda lead, m_: pl.BlockSpec((lead, m_, eb), lambda i: (0, 0, i))
 
+    def per_channel(*parts):
+        joined = jnp.concatenate([p.astype(F32) for p in parts], axis=0)
+        return jnp.pad(joined, ((0, -joined.shape[0] % 8), (0, 0)))
+
+    conv_chan = per_channel(convolution_taps, convolution_bias[None])
+    state_chan = per_channel(decay_rates, step_size_bias[None], skip[None])
+
     conv_next, u = pl.pallas_call(
         conv_kernel,
         name="conv_step",
         grid=grid,
         out_shape=(sds((taps, chans, reqs), BF16), sds((chans, reqs), BF16)),
         in_specs=[rowb(reqs), mid(taps, reqs), lastb(taps, buffers), whole(buffers, reqs),
-                  whole(1, reqs), rowb(taps + 1), rowb(1)],
+                  whole(1, reqs), pl.BlockSpec((conv_chan.shape[0], eb), lambda i: (0, i))],
         out_specs=(mid(taps, reqs), rowb(reqs)),
         compiler_params=pltpu.CompilerParams(vmem_limit_bytes=LIMIT),
-    )(x_in, convolution_cache, land_conv, pick, hit, convolution_taps.astype(F32).T,
-      convolution_bias.astype(F32)[:, None])
+    )(x_in, convolution_cache, land_conv, pick, hit, conv_chan)
 
     outs = rank + 2 * states
     mix_part = dot0(u, step_input_projection).astype(BF16).reshape(m, 2, share, outs)
@@ -534,12 +538,12 @@
         name="state_step",
         grid=grid,
         out_shape=(sds((states, chans, reqs), BF16), sds((chans, reqs), BF16)),
-        in_specs=[whole(outs, reqs), pl.BlockSpec((rank, eb), lambda i: (0, i)), rowb(1),
-                  rowb(states), rowb(1), rowb(reqs), rowb(reqs), mid(states, reqs), lastb(states, buffers),
+        in_specs=[whole(outs, reqs), pl.BlockSpec((rank, eb), lambda i: (0, i)),
+                  pl.BlockSpec((state_chan.shape[0], eb), lambda i: (0, i)), rowb(reqs), rowb(reqs), mid(states, reqs), lastb(states, buffers),
                   whole(buffers, reqs), whole(1, reqs)],
         out_specs=(mid(states, reqs), rowb(reqs)),
         compiler_params=pltpu.CompilerParams(vmem_limit_bytes=LIMIT),
-    )(mixed_in, step_size_projection, step_size_bias[:, None], decay_rates.T, skip[:, None], u,
+    )(mixed_in, step_size_projection, state_chan, u,
       gate_in, recurrent_cache, land_ssm, pick, hit)
 
     down = adapter_down_maps.transpose(0, 2, 1).reshape(tenants * low_rank, chans)

time: 197 us -> 193 us (0.980)
  local copies, waits for them, and re-layouts: 17.8 us -> 11.5 us
    broadcast_in_dim x3 -> x0, local copies, waits for them, and re-layouts: 3.9 us -> none  [the longest x1 1.53 us: local(): step_size_bias[:, None]]
    unnamed x5 -> x4, local copies, waits for them, and re-layouts: 4.44 us -> 2.86 us
where the time goes in v3:
time: 193 us; the launch traced here: 192 us
  Pallas kernels  173 us (90%)
  local copies, waits for them, and re-layouts  11.5 us (6%)
  matrix products  3.61 us (2%)
  other arithmetic  2.7 us (1%)
    pallas_call x1, Pallas kernels, local(): pl.pallas_call(functools.partial(gather_kernel, n, snake), name='gather_p...  71 us
    pallas_call x1, Pallas kernels, local(): pl.pallas_call(functools.partial(scatter_kernel, n, snake), name='project...  61.7 us
    pallas_call x1, Pallas kernels, local(): pl.pallas_call(functools.partial(mix_kernel, n, rank), name='mix_sum', ou...  22.8 us
    pallas_call x1, Pallas kernels, local(): pl.pallas_call(state_kernel, name='state_step', grid=grid, out_shape=(sds...  13.1 us
    pallas_call x1, Pallas kernels, local(): pl.pallas_call(conv_kernel, name='conv_step', grid=grid, out_shape=(sds((...  4.69 us

profile of v3, /device:TPU:0, one launch (start us, length us, event | category | flops | bytes accessed | tf_op | source)
XLA Modules:
  0.0 191.8 jit_solution(8601443997679977253)
XLA Ops:
  0.6 0.0 copy-start
  0.6 0.7 convert_element_type.20
  1.4 1.3 fusion.5.chan_ref
  2.7 2.1 %fusion.7 = (f32[512]{0:T(512)}, bf16[32,512]{1,0:T(8,128)(2,1)}) fusion(s32[32]{0:T(128)} %param.41, s32[32]{0:T(128)} %param.40), kind=kOutput, calls=%fused_computation.17 | convolution fusion | flops 1098240 | bytes 35072 | tf_op jit(solution)/shard_map/dot_general | solution.py:492
  4.8 1.4 select_maximum_fusion.chan_ref
  6.2 1.0 copy.27
  7.2 0.1 reshape.34
  7.3 0.1 copy.38
  7.4 0.7 pad.14.conv_hbm
  8.1 71.0 %gather_project.1 = (f32[512,512]{1,0:T(8,128)}, f32[512,512]{1,0:T(8,128)}, bf16[16,2,16,512]{3,2,1,0:T(8,128)(2,1)}, bf16[16,16,512]{2,1,0:T(8,128)(2,1)}) custom-call(bf16[512,512]{1,0:T(8,128)(2,1)} %h_ref.1, bf16[8192,512]{1,0:T(8,128)(2,1)} %wx_hbm.1, bf16[8192,512]{1,0:T(8,128)(2,1)} %wg_hbm.1, bf16[2,16,8192]{2,1,0:T(8,128)(2,1)} %ssm_hbm.1, ...), custom_call_target="tpu_custom_call" | custom-call | tf_op jit(solution)/shard_map/gather_project/pallas_call | solution.py:474
  79.2 0.9 slice.3
  80.1 0.1 reshape.35
  80.2 0.7 copy.39
  80.8 2.1 %copy.37 = bf16[32,16,512]{2,0,1:T(8,128)(2,1)} copy(bf16[32,16,512]{2,1,0:T(8,128)(2,1)} %bitcast.31) | data formatting | bytes 1048576 | tf_op jit(solution)/shard_map/reshape | solution.py:490
  83.0 4.7 %conv_step.1 = (bf16[3,512,512]{2,1,0:T(8,128)(2,1)}, bf16[512,512]{1,0:T(8,128)(2,1)}) custom-call(f32[512,512]{1,0:T(8,128)} %get-tuple-element.11.x_ref, bf16[3,512,512]{2,1,0:T(8,128)(2,1)} %cache_ref.2, bf16[3,32,512]{2,1,0:T(8,128)(2,1)} %bitcast.32, bf16[32,512]{1,0:T(8,128)(2,1)} %get-tuple-element.20.pick_ref, f32[1,512]{1,0:T(1,128)} %bitcast.33, ...), custom_call_target="tpu_custom_call" | custom-call | tf_op jit(solution)/shard_map/conv_step/pallas_call | solution.py:511
  87.7 0.0 copy-done
  87.7 1.5 convolution_convert_fusion
  89.2 1.1 copy.30
  90.2 22.8 %mix_sum.1 = bf16[16,32,544]{2,1,0:T(8,128)(2,1)} custom-call(bf16[8,2,32,544]{3,2,1,0:T(8,128)(2,1)} %bitcast.24, f32[1,512]{1,0:T(1,128)} %bitcast.35), custom_call_target="tpu_custom_call" | custom-call | tf_op jit(solution)/shard_map/mix_sum/pallas_call | solution.py:524
  113.0 2.1 %copy.31 = bf16[512,544]{0,1:T(8,128)(2,1)} copy(bf16[512,544]{1,0:T(8,128)(2,1)} %bitcast.25) | data formatting | bytes 1114112 | tf_op jit(solution)/shard_map/reshape | solution.py:534
  115.1 13.1 %state_step.1 = (bf16[16,512,512]{2,1,0:T(8,128)(2,1)}, bf16[512,512]{1,0:T(8,128)(2,1)}) custom-call(bf16[544,512]{1,0:T(8,128)(2,1)} %bitcast.26, bf16[512,512]{1,0:T(8,128)(2,1)} %proj_ref.1, f32[24,512]{1,0:T(8,128)} %select_maximum_fusion.chan_ref, bf16[512,512]{1,0:T(8,128)(2,1)} %get-tuple-element.13.u_ref, f32[512,512]{1,0:T(8,128)} %get-tuple-element.14.gate_ref, ...), custom_call_target="tpu_custom_call" | custom-call | tf_op jit(solution)/shard_map/state_step/pallas_call | solution.py:536
  128.2 61.7 %project_scatter.1 = bf16[512,512]{1,0:T(8,128)(2,1)} custom-call(bf16[512,512]{1,0:T(8,128)(2,1)} %get-tuple-element.16.y_ref, bf16[512,8192]{1,0:T(8,128)(2,1)} %w_hbm.1, bf16[1024,512]{1,0:T(8,128)(2,1)} %bitcast.28, bf16[1024,512]{1,0:T(8,128)(2,1)} %bitcast.29, s32[1,512]{1,0:T(1,128)} %bitcast.36), custom_call_target="tpu_custom_call" | custom-call | tf_op jit(solution)/shard_map/project_scatter/pallas_call | solution.py:553
  189.9 1.9 copy.41
Async XLA Ops:
  0.6 87.0 %copy-start = (bf16[512,544]{0,1:T(8,128)(2,1)S(1)}, bf16[512,544]{0,1:T(8,128)(2,1)}, u32[]{:S(2)}) copy-start(bf16[512,544]{0,1:T(8,128)(2,1)} %param.26) | copy-start | bytes 1671172
